TPU v7x, 256 devices: a whole 4x4x8 slice. The times are simulated.
256 devices in a mesh: gx: 16 (over x, y_lo, core), gy: 16 (over y_hi, z).
Axes of the slice: x: 4, y: 4 (y_hi: 2, y_lo: 2; y = y_hi * 2 + y_lo), z: 8, core: 2. Of those that a mesh axis runs over, the one named last changes fastest.
Arguments:
- tokens: bfloat16 [1024, 8192], P('gx'), may hold values from -6 to 6
- gate_weight: bfloat16 [8192, 28672], P('gx', 'gy'), may hold values from -0.0625 to 0.0625
- up_weight: bfloat16 [8192, 28672], P('gx', 'gy'), may hold values from -0.0625 to 0.0625
- down_weight: bfloat16 [28672, 8192], P('gy', 'gx'), may hold values from -0.03125 to 0.03125
- valid_counts: int32 [16], replicated, may hold values from 1 to 64, 768 in all
Outputs:
- mixed: float32 [1024, 8192], P('gy', 'gx')
Inputs may be any that keep to these rules, and one draw needn't show every extreme that they name: valid_counts sum to 768 and the largest equals 64.
All inputs are finite; a program needn't handle non-finite values.
Results may differ from a plain program's by a relative error of at most 0.0029.
Values may be sent and summed in bfloat16 or wider, within the bound.
A program may use at most 128 MiB of HBM per device.

v0:
```python
import jax
import jax.numpy as jnp
from jax import lax
from jax.sharding import PartitionSpec as P


def body(tokens, gate_weight, up_weight, down_weight, valid_counts):
    row_total = tokens.shape[0]
    hidden_width = gate_weight.shape[1]
    group_index = lax.axis_index("gx")
    columns = lax.all_to_all(tokens, "gx", split_axis=1, concat_axis=0, tiled=True)
    paired_weights = jnp.concatenate((gate_weight, up_weight), axis=1)
    summed = lax.psum_scatter(
        jnp.dot(columns, paired_weights, preferred_element_type=jnp.float32),
        "gx",
        scatter_dimension=0,
        tiled=True,
    )
    gate_sum = summed[:, :hidden_width]
    up_sum = summed[:, hidden_width:]
    live_rows = (jnp.arange(row_total, dtype=jnp.int32) < valid_counts[group_index]).astype(
        jnp.int32
    )
    hidden = jnp.where(
        live_rows[:, None] == 1, jax.nn.silu(gate_sum) * up_sum, jnp.float32(0.0)
    ).astype(jnp.bfloat16)
    partials = jnp.dot(
        lax.all_gather(hidden, "gx", axis=0, tiled=True),
        down_weight,
        preferred_element_type=jnp.float32,
    )
    return lax.psum_scatter(partials, "gy", scatter_dimension=0, tiled=True)


def solution(mesh):
    in_specs = (P("gx", None), P("gx", "gy"), P("gx", "gy"), P("gy", "gx"), P())
    out_specs = P("gy", "gx")
    return jax.shard_map(body, mesh=mesh, in_specs=in_specs, out_specs=out_specs, check_vma=False)
```

profile of v0, /device:TPU:80, one launch (start us, length us, event | category | flops | bytes accessed | tf_op | source)
XLA Modules:
  0.0 472.6 jit_solution(9262288671605364639)
XLA Ops:
  6.5 0.0 copy-start
  6.5 0.0 reduce-scatter.7.cloned.1.call-start
  6.5 0.0 copy-start.1
  6.5 0.0 copy-start.2
  6.5 1.5 copy.16
  8.0 21.5 %all_to_all.19 = bf16[64,16,512]{2,0,1:T(8,128)(2,1)S(1)} all-to-all(bf16[64,16,512]{2,0,1:T(8,128)(2,1)S(1)} %bitcast.14), channel_id=1, replica_groups=mesh['gx'=16,'gy'=16] {'gx'}, dimensions={1} | all-to-all | bytes 2097152 | tf_op jit(solution)/shard_map/all_to_all | solution.py:11
  29.6 0.0 copy-done.1
  29.6 0.0 copy-done.2
  29.6 7.3 %convolution_bitcast_fusion = f32[1024,3584]{0,1:T(8,128)} fusion(bf16[1024,512]{1,0:T(8,128)(2,1)S(1)} %bitcast.16, bf16[512,1792]{1,0:T(8,128)(2,1)S(1)} %copy-done.1, bf16[512,1792]{1,0:T(8,128)(2,1)S(1)} %copy-done.2), kind=kOutput, calls=%fused_computation | convolution fusion | flops 3765436416 | bytes 19398656 | tf_op jit(solution)/shard_map/dot_general | solution.py:14
  36.9 14.4 %copy.12 = f32[1024,3584]{1,0:T(8,128)} copy(f32[1024,3584]{0,1:T(8,128)} %convolution_bitcast_fusion) | data formatting | bytes 29360128
  51.3 0.0 copy-start.3
  51.3 0.0 reduce-scatter.7.cloned.1.call-update
  51.3 0.0 all-gather.2.cloned.1.call-start
  51.3 0.6 copy-done.3
  51.9 0.6 dynamic_slice.3
  52.5 0.6 fusion.5
  53.2 156.3 %reduce-scatter.7.cloned.1.call-done = f32[64,3584]{1,0:T(8,128)} async-done(((f32[1024,3584]{1,0:T(8,128)}), f32[64,3584]{1,0:T(8,128)}) %reduce-scatter.7.cloned.1.call-update) | async-done | bytes 917520 | tf_op jit(solution)/shard_map/reduce_scatter | solution.py:13
  209.5 2.0 fusion.4
  211.4 0.0 all-gather.2.cloned.1.call-update
  211.5 0.0 reduce-scatter.5.cloned.1.call-start
  211.5 43.4 %all-gather.2.cloned.1.call-done = bf16[1024,1792]{1,0:T(8,128)(2,1)} async-done(((bf16[64,1792]{1,0:T(8,128)(2,1)}), bf16[1024,1792]{1,0:T(8,128)(2,1)}) %all-gather.2.cloned.1.call-update) | async-done | bytes 3670032 | tf_op jit(solution)/shard_map/all_gather | solution.py:28
  254.9 0.0 copy-done
  254.9 5.4 %fusion.7 = f32[1024,512]{1,0:T(8,128)} fusion(bf16[1024,1792]{1,0:T(8,128)(2,1)} %all-gather.2.cloned.1.call-done, bf16[1792,512]{1,0:T(8,128)(2,1)S(1)} %copy-done), kind=kOutput, calls=%fused_computation.11 | convolution fusion | flops 1879048192 | bytes 7602176 | tf_op jit(solution)/shard_map/dot_general | solution.py:27
  260.3 0.0 reduce-scatter.5.cloned.1.call-update
  260.3 205.8 %reduce-scatter.5.cloned.1.call-done = f32[64,512]{1,0:T(8,128)} async-done(((f32[1024,512]{1,0:T(8,128)}), f32[64,512]{1,0:T(8,128)}) %reduce-scatter.5.cloned.1.call-update) | async-done | bytes 131088 | tf_op jit(solution)/shard_map/reduce_scatter | solution.py:32
Async XLA Ops:
  6.5 248.3 %copy-start = (bf16[1792,512]{1,0:T(8,128)(2,1)S(1)}, bf16[1792,512]{1,0:T(8,128)(2,1)}, u32[]{:S(2)}) copy-start(bf16[1792,512]{1,0:T(8,128)(2,1)} %param.8) | copy-start | bytes 5505028
  6.5 202.9 %reduce-scatter.7.cloned.1.call-start = ((), (), s32[]{:S(2)}) async-start(), calls=%async_computation.5 | async-start | bytes 15597568 | tf_op jit(solution)/shard_map/reduce_scatter | solution.py:13
  6.5 23.0 %copy-start.1 = (bf16[512,1792]{1,0:T(8,128)(2,1)S(1)}, bf16[512,1792]{1,0:T(8,128)(2,1)}, u32[]{:S(2)}) copy-start(bf16[512,1792]{1,0:T(8,128)(2,1)} %param.7) | copy-start | bytes 5505028
  6.5 23.0 %copy-start.2 = (bf16[512,1792]{1,0:T(8,128)(2,1)S(1)}, bf16[512,1792]{1,0:T(8,128)(2,1)}, u32[]{:S(2)}) copy-start(bf16[512,1792]{1,0:T(8,128)(2,1)} %param.6) | copy-start | bytes 5505028
  51.3 0.7 copy-start.3
  51.3 203.6 %all-gather.2.cloned.1.call-start = ((), (), s32[]{:S(2)}) async-start(), calls=%async_computation.3 | async-start | bytes 3899392 | tf_op jit(solution)/shard_map/all_gather | solution.py:28
  211.5 254.6 %reduce-scatter.5.cloned.1.call-start = ((), (), s32[]{:S(2)}) async-start(), calls=%async_computation.4 | async-start | bytes 2228224 | tf_op jit(solution)/shard_map/reduce_scatter | solution.py:32
Sparse Core Ops, SparseCore 0:
  51.4 158.0 reduce-scatter.6
  211.6 43.2 all-gather.1
  260.4 205.6 reduce-scatter.4
where the time goes:
time: 477 us; the launch traced here: 473 us
  waiting for transfers between devices  405 us (85%)
  blocking collectives  21.5 us (5%)
  local copies, waits for them, and re-layouts  17 us (4%)
  between operations  13.1 us (3%)
  matrix products  12.7 us (3%)
    reduce_scatter x1, waiting for transfers between devices, body(): return lax.psum_scatter(partials, 'gy', scatter_dimension=0, tiled=True)  206 us
    reduce_scatter x1, waiting for transfers between devices, body(): lax.psum_scatter(jnp.dot(columns, paired_weights, preferred_element_type=...  156 us
    all_gather x1, waiting for transfers between devices, body(): lax.all_gather(hidden, 'gx', axis=0, tiled=True)  43.4 us
    all_to_all x1, blocking collectives, body(): lax.all_to_all(tokens, 'gx', split_axis=1, concat_axis=0, tiled=True)  21.5 us
    unnamed x9, local copies, waits for them, and re-layouts  15 us
  transfers between devices with their start and end apart: 3, of which 3 were waited for; matrix products, arithmetic and copies ran while one was open for 0% of the time, Pallas kernels for 0%

commit v1 on v0

v1 whole, which is shorter than its diff:
```python
import functools

import jax
import jax.numpy as jnp
from jax import lax
from jax.experimental import pallas as pl
from jax.experimental.pallas import tpu as pltpu
from jax.sharding import PartitionSpec as P

MESH = pl.DeviceIdType.MESH
BF16, F32, I16, I32 = jnp.bfloat16, jnp.float32, jnp.int16, jnp.int32

N = 16
CHIPS = 8
ROWS = 64
LIVE = 768
CHUNKS = 3
M = LIVE // CHUNKS
MC = M // CHIPS
MZ = M // N
SPAN = 8
WINDOW = 20
DEST = 5
FULL = 32000.0


def aligned(index, unit):
    return pl.ds(pl.multiple_of(index * unit, unit), unit)


def kernel(
    counts, tokens, gate, up, down, out,
    tok, wg, wu, wd, xs, qs, qr, hid, part, zs, zr, zsum, fin,
    local_sem, tok_send, tok_recv, w_send, w_recv, x_send, x_recv,
    q_send, q_recv, h_send, h_recv, f_send, f_recv, z_send, z_recv, e_send, e_recv, e_local,
):
    gx, gy = lax.axis_index("gx"), lax.axis_index("gy")
    chip, core = gx // 2, gx % 2
    depth = gate.shape[0]
    half = gate.shape[1] // 2
    width = down.shape[1]
    sibling = (gx + 1 - 2 * core, gy)

    def remote(src, dst, send, recv, device):
        return pltpu.make_async_remote_copy(
            src_ref=src, dst_ref=dst, send_sem=send, recv_sem=recv, device_id=device, device_id_type=MESH
        )

    def peer_chip(d):
        return (chip + d) % CHIPS

    mine = aligned(core, half)
    my_rows = aligned(core, depth)
    local = [
        pltpu.make_async_copy(tokens.at[:, aligned(gx, depth)], tok.at[aligned(gx, ROWS)], local_sem.at[0]),
        pltpu.make_async_copy(gate.at[:, mine], wg.at[my_rows], local_sem.at[1]),
        pltpu.make_async_copy(up.at[:, mine], wu.at[my_rows], local_sem.at[2]),
        pltpu.make_async_copy(down, wd, local_sem.at[3]),
    ]
    for copy in local:
        copy.start()
    fin[...] = jnp.zeros_like(fin)

    barrier = pltpu.get_barrier_semaphore()

    def greet(d, carry):
        pl.semaphore_signal(barrier, inc=1, device_id=((gx + d) % N, gy), device_id_type=MESH)
        pl.semaphore_signal(barrier, inc=1, device_id=(gx, (gy + d) % N), device_id_type=MESH)
        return carry

    lax.fori_loop(1, N, greet, 0)
    pl.semaphore_wait(barrier, 2 * (N - 1))

    def token_copy(d):
        to = (gx + d) % N
        return remote(
            tokens.at[:, aligned(to, depth)], tok.at[aligned(gx, ROWS)], tok_send.at[d], tok_recv.at[gx], (to, gy)
        )

    def start_tokens(d, carry):
        token_copy(d).start()
        return carry

    lax.fori_loop(1, N, start_tokens, 0)

    theirs = aligned(1 - core, half)
    weights = [
        remote(gate.at[:, theirs], wg.at[my_rows], w_send.at[0], w_recv.at[0], sibling),
        remote(up.at[:, theirs], wu.at[my_rows], w_send.at[1], w_recv.at[1], sibling),
    ]
    for copy in weights:
        copy.start()

    count = [counts[g] for g in range(N)]
    first = [jnp.int32(0)]
    for g in range(N - 1):
        first.append(first[-1] + count[g])

    def wait_tokens(g, carry):
        @pl.when(g != gx)
        def _():
            remote(tok.at[aligned(g, ROWS)], tok.at[aligned(g, ROWS)], tok_send.at[0], tok_recv.at[g], (g, gy)).wait_recv()

        return carry

    def compact(k):
        lane = lax.broadcasted_iota(I32, (1, SPAN * ROWS), 1)
        place = jnp.full((1, SPAN * ROWS), -1, I32)
        for i in range(SPAN):
            g = 4 * k + i
            slot = lane - ROWS * i
            place = jnp.where((slot >= 0) & (slot < count[g]), slot + (first[g] - M * k), place)
        row = lax.broadcasted_iota(I32, (M, SPAN * ROWS), 0)
        pick = jnp.where(row == place, 1.0, 0.0).astype(BF16)
        rows = jnp.dot(pick, tok[pl.ds(4 * k * ROWS, SPAN * ROWS), :], preferred_element_type=F32)
        xs[k, :, my_rows] = rows.astype(BF16)

    def x_copy(k):
        return remote(xs.at[k, :, my_rows], xs.at[k, :, my_rows], x_send.at[k], x_recv.at[k], sibling)

    local[0].wait()
    for k in range(CHUNKS):
        lax.fori_loop(0 if k == 0 else 4 * k + 4, 4 * k + 8, wait_tokens, 0)
        compact(k)
        x_copy(k).start()

    for copy in local[1:3]:
        copy.wait()
    for copy in weights:
        copy.wait_recv()

    def q_copy(k, d):
        to = peer_chip(d)
        return remote(
            qs.at[k, aligned(to, MC)], qr.at[k, chip], q_send.at[k, d], q_recv.at[k, chip], (2 * to + core, gy)
        )

    def project(k):
        x = xs[k]
        g = jnp.dot(x, wg[...], preferred_element_type=F32)
        u = jnp.dot(x, wu[...], preferred_element_type=F32)
        top = jnp.maximum(jnp.max(jnp.abs(g), axis=1, keepdims=True), jnp.max(jnp.abs(u), axis=1, keepdims=True))
        level = jnp.ceil(jnp.log(jnp.maximum(top, 1e-30)) * (64.0 / 0.6931471805599453)) + 1.0
        to_code = FULL * jnp.exp2(level * (-1.0 / 64.0))
        qs[k, :, :half] = jnp.round(g * to_code).astype(I32).astype(I16)
        qs[k, :, half : 2 * half] = jnp.round(u * to_code).astype(I32).astype(I16)
        qs[k, :, 2 * half :] = jnp.broadcast_to(level.astype(I32), (M, 128)).astype(I16)

    for k in range(CHUNKS):
        x_copy(k).wait_recv()
        project(k)

        def start_sums(d, carry, k=k):
            q_copy(k, d).start()
            return carry

        lax.fori_loop(1, CHIPS, start_sums, 0)

    def h_copy(k, d):
        to = peer_chip(d)
        block = hid.at[k, aligned(chip, MC), mine]
        return remote(block, block, h_send.at[k, d], h_recv.at[k, chip], (2 * to + core, gy))

    def decode(block):
        scale = jnp.exp2(block[:, 2 * half :].astype(I32).astype(F32)[:, :1] * (1.0 / 64.0)) * (1.0 / FULL)
        return block[:, : 2 * half].astype(I32).astype(F32) * scale

    def activate(k):
        total = decode(qs[k, aligned(chip, MC), :])
        for d in range(1, CHIPS):
            source = peer_chip(d)
            remote(qr.at[k, source], qr.at[k, source], q_send.at[k, 0], q_recv.at[k, source], sibling).wait_recv()
            total = total + decode(qr[k, source])
        g, u = total[:, :half], total[:, half:]
        hid[k, aligned(chip, MC), mine] = (g / (1.0 + jnp.exp(-g)) * u).astype(BF16)

        def start_hidden(d, carry):
            h_copy(k, d).start()
            return carry

        lax.fori_loop(1, CHIPS, start_hidden, 0)

    def f_copy(k):
        return remote(hid.at[k, :, mine], hid.at[k, :, mine], f_send.at[k], f_recv.at[k], sibling)

    def forward(k):
        def wait_hidden(d, carry):
            source = peer_chip(d)
            block = hid.at[k, aligned(source, MC), mine]
            remote(block, block, h_send.at[k, 0], h_recv.at[k, source], sibling).wait_recv()
            return carry

        lax.fori_loop(1, CHIPS, wait_hidden, 0)
        f_copy(k).start()

    def z_copy(k, d):
        to = (gy + d) % N
        return remote(zs.at[k, aligned(to, MZ)], zr.at[k, gy], z_send.at[k, d], z_recv.at[k, gy], (gx, to))

    def contract(k):
        f_copy(k).wait_recv()
        o = jnp.dot(hid[k], wd[...], preferred_element_type=F32)
        part[k] = o
        zs[k] = o.astype(BF16)

        def start_out(d, carry):
            z_copy(k, d).start()
            return carry

        lax.fori_loop(1, N, start_out, 0)

    def e_copy(k, i):
        to = 4 * k + gy // 4 + i
        place = (N * k + gy) - 4 * to + 16
        return to, place

    def collect(k):
        def add(d, total):
            source = (gy + d) % N
            remote(zr.at[k, source], zr.at[k, source], z_send.at[k, 0], z_recv.at[k, source], sibling).wait_recv()
            return total + zr[k, source].astype(F32)

        zsum[k] = lax.fori_loop(1, N, add, part[k, aligned(gy, MZ), :])
        for i in range(DEST):
            to, place = e_copy(k, i)

            @pl.when(to == gy)
            def _():
                pltpu.make_async_copy(zsum.at[k], fin.at[place], e_local.at[k]).start()

            @pl.when(to != gy)
            def _():
                remote(zsum.at[k], fin.at[place], e_send.at[k, i], e_recv.at[place], (gx, to)).start()

    activate(0)
    activate(1)
    forward(0)
    local[3].wait()
    activate(2)
    contract(0)
    forward(1)
    contract(1)
    forward(2)
    collect(0)
    contract(2)
    collect(1)
    collect(2)

    def wait_rows(place, carry):
        block = 4 * gy - 16 + place

        @pl.when((block >= 0) & (block < N * CHUNKS) & (block % N != gy))
        def _():
            remote(zsum.at[0], fin.at[place], e_send.at[0, 0], e_recv.at[place], sibling).wait_recv()

        return carry

    lax.fori_loop(0, WINDOW, wait_rows, 0)
    for k in range(CHUNKS):
        for i in range(DEST):
            to, place = e_copy(k, i)

            @pl.when(to == gy)
            def _():
                pltpu.make_async_copy(zsum.at[k], fin.at[place], e_local.at[k]).wait()

    my_count, my_first = jnp.int32(0), jnp.int32(0)
    for g in range(N):
        my_count = my_count + jnp.where(g == gy, count[g], 0)
        my_first = my_first + jnp.where(g < gy, count[g], 0)
    slot = lax.broadcasted_iota(I32, (ROWS, WINDOW * MZ), 0)
    live = lax.broadcasted_iota(I32, (ROWS, WINDOW * MZ), 1) + (ROWS * gy - 256) - my_first
    pick = jnp.where((live == slot) & (slot < my_count), 1.0, 0.0).astype(BF16)
    rest = fin[...].reshape(WINDOW * MZ, width)
    total = jnp.zeros((ROWS, width), F32)
    for _ in range(3):
        term = rest.astype(BF16)
        total = total + jnp.dot(pick, term, preferred_element_type=F32)
        rest = rest - term.astype(F32)
    out[...] = total

    for copy in weights:
        copy.wait_send()

    def sent_tokens(d, carry):
        token_copy(d).wait_send()
        return carry

    lax.fori_loop(1, N, sent_tokens, 0)
    for k in range(CHUNKS):
        x_copy(k).wait_send()
        f_copy(k).wait_send()

        def sent_chip(d, carry, k=k):
            q_copy(k, d).wait_send()
            h_copy(k, d).wait_send()
            return carry

        def sent_out(d, carry, k=k):
            z_copy(k, d).wait_send()
            return carry

        lax.fori_loop(1, CHIPS, sent_chip, 0)
        lax.fori_loop(1, N, sent_out, 0)
        for i in range(DEST):
            to, place = e_copy(k, i)

            @pl.when(to != gy)
            def _():
                remote(zsum.at[k], fin.at[place], e_send.at[k, i], e_recv.at[place], (gx, to)).wait_send()


def body(tokens, gate, up, down, counts):
    depth, hidden = gate.shape
    width = down.shape[1]
    half = hidden // 2
    code = 2 * half + 128
    dma = pltpu.SemaphoreType.DMA
    any_space = pl.BlockSpec(memory_space=pl.ANY)
    return pl.pallas_call(
        kernel,
        out_shape=jax.ShapeDtypeStruct((ROWS, width), F32),
        in_specs=[pl.BlockSpec(memory_space=pltpu.SMEM)] + [any_space] * 4,
        out_specs=pl.BlockSpec(memory_space=pltpu.VMEM),
        scratch_shapes=[
            pltpu.VMEM((N * ROWS, depth), BF16),
            pltpu.VMEM((2 * depth, half), BF16),
            pltpu.VMEM((2 * depth, half), BF16),
            pltpu.VMEM((hidden, width), BF16),
            pltpu.VMEM((CHUNKS, M, 2 * depth), BF16),
            pltpu.VMEM((CHUNKS, M, code), I16),
            pltpu.VMEM((CHUNKS, CHIPS, MC, code), I16),
            pltpu.VMEM((CHUNKS, M, hidden), BF16),
            pltpu.VMEM((CHUNKS, M, width), F32),
            pltpu.VMEM((CHUNKS, M, width), BF16),
            pltpu.VMEM((CHUNKS, N, MZ, width), BF16),
            pltpu.VMEM((CHUNKS, MZ, width), F32),
            pltpu.VMEM((WINDOW, MZ, width), F32),
            dma((4,)),
            dma((N,)), dma((N,)),
            dma((2,)), dma((2,)),
            dma((CHUNKS,)), dma((CHUNKS,)),
            dma((CHUNKS, CHIPS)), dma((CHUNKS, CHIPS)),
            dma((CHUNKS, CHIPS)), dma((CHUNKS, CHIPS)),
            dma((CHUNKS,)), dma((CHUNKS,)),
            dma((CHUNKS, N)), dma((CHUNKS, N)),
            dma((CHUNKS, DEST)), dma((WINDOW,)),
            dma((CHUNKS,)),
        ],
        compiler_params=pltpu.CompilerParams(
            collective_id=0, has_side_effects=True, vmem_limit_bytes=56 * 2**20
        ),
        name="swiglu",
    )(counts, tokens, gate, up, down)


def solution(mesh):
    in_specs = (P("gx", None), P("gx", "gy"), P("gx", "gy"), P("gy", "gx"), P())
    out_specs = P("gy", "gx")
    return jax.shard_map(body, mesh=mesh, in_specs=in_specs, out_specs=out_specs, check_vma=False)
```

time: 477 us -> 113 us (0.24)
  waiting for transfers between devices: 405 us -> 0 us
  Pallas kernels: 0 us -> 111 us
  blocking collectives: 21.5 us -> 0 us
  local copies, waits for them, and re-layouts: 17 us -> 1.57 us
  between operations: 13.1 us -> 0.01 us
  matrix products: 12.7 us -> 0 us
    reduce_scatter x2 -> x0, waiting for transfers between devices: 362 us -> none  [the longest x1 206 us: body(): return lax.psum_scatter(partials, 'gy', scatter_dimension=0, tiled=True)]
    pallas_call x0 -> x1, Pallas kernels: none -> 111 us  [body(): pl.pallas_call(kernel, out_shape=jax.ShapeDtypeStruct((ROWS, width), F32)...]
    all_gather x1 -> x0, waiting for transfers between devices: 43.4 us -> none  [body(): lax.all_gather(hidden, 'gx', axis=0, tiled=True)]
    all_to_all x1 -> x0, blocking collectives: 21.5 us -> none  [body(): lax.all_to_all(tokens, 'gx', split_axis=1, concat_axis=0, tiled=True)]
    unnamed x9 -> x1, local copies, waits for them, and re-layouts: 15 us -> 1.57 us
    dot_general x2 -> x0, matrix products: 12.7 us -> none  [the longest x1 7.32 us: body(): jnp.dot(columns, paired_weights, preferred_element_type=jnp.float32)]
  transfers between devices with their start and end apart: 3 -> 0, of which waited for: 3 -> 0; matrix products, arithmetic and copies ran while one was open for 0% -> 0% of each run, Pallas kernels for 0% -> 0%
where the time goes in v1:
time: 113 us
  Pallas kernels  111 us (98%)
  local copies, waits for them, and re-layouts  1.57 us (1%)
    pallas_call x1, Pallas kernels, body(): pl.pallas_call(kernel, out_shape=jax.ShapeDtypeStruct((ROWS, width), F32)...  111 us

profile of v1, /device:TPU:80, one launch (start us, length us, event | category | flops | bytes accessed | tf_op | source)
XLA Modules:
  0.0 112.9 jit_solution(132893625083968526)
XLA Ops:
  0.0 111.4 %swiglu.1 = f32[64,512]{1,0:T(8,128)} custom-call(s32[16]{0:T(128)} %counts.1, bf16[64,8192]{1,0:T(8,128)(2,1)} %tokens.1, bf16[512,1792]{1,0:T(8,128)(2,1)} %gate.1, bf16[512,1792]{1,0:T(8,128)(2,1)} %up.1, bf16[1792,512]{1,0:T(8,128)(2,1)} %down.1), custom_call_target="tpu_custom_call" | custom-call | tf_op jit(solution)/shard_map/swiglu/pallas_call | solution.py:320
  111.4 1.6 %copy.7 = f32[64,512]{1,0:T(8,128)} copy(f32[64,512]{1,0:T(8,128)} %swiglu.1) | data formatting | bytes 262144

commit v2 on v1

v2 whole, which is shorter than its diff:
```python
import functools

import jax
import jax.numpy as jnp
from jax import lax
from jax.experimental import pallas as pl
from jax.experimental.pallas import tpu as pltpu
from jax.sharding import PartitionSpec as P

MESH = pl.DeviceIdType.MESH
BF16, F32, I16, I32 = jnp.bfloat16, jnp.float32, jnp.int16, jnp.int32

N = 16
CHIPS = 8
NX = 4
ROWS = 64
LIVE = 768
TYPES = (0, 1, 0, 0, 1, 0)
CHUNKS = len(TYPES)
M = LIVE // CHUNKS
MC = M // CHIPS
MZ = 16
OWNERS = M // MZ
ORDER = (
    (0, 0), (0, 1), (0, 2), (0, 3), (0, 4), (0, 5), (1, 0), (1, 1), (1, 2), (1, 4), (2, 0), (1, 3),
    (2, 2), (3, 0), (1, 5), (2, 3), (2, 1), (3, 2), (2, 4), (4, 0), (2, 5), (3, 1), (3, 3), (5, 0),
    (4, 2), (3, 5), (3, 4), (5, 2), (4, 1), (4, 3), (5, 1), (5, 3), (6, 0), (4, 4), (4, 5), (5, 4),
    (6, 2), (5, 5), (6, 1), (6, 3), (6, 4), (6, 5),
)
SPAN = 6
WINDOW = 20
DEST = 5
FULL = 32000.0


def aligned(index, unit):
    return pl.ds(pl.multiple_of(index * unit, unit), unit)


def kernel(
    counts, tokens, gate, up, down, out,
    tok, wg, wu, wd, xs, qs, q1, qm, q2, hid, part, zs, zr, ecode, fin,
    local_sem, tok_send, tok_recv, w_send, w_recv, x_send, x_recv,
    a_send, a_recv, b_send, b_recv, h_send, h_recv, g_send, g_recv, f_send, f_recv,
    z_send, z_recv, e_send, e_recv, e_local,
):
    gx, gy = lax.axis_index("gx"), lax.axis_index("gy")
    along_x, along_y, core = gx // 4, gx // 2 % 2, gx % 2
    depth = gate.shape[0]
    half = gate.shape[1] // 2
    width = down.shape[1]
    sibling = (gx + 1 - 2 * core, gy)
    across = (gx + 2 - 4 * along_y, gy)

    def remote(src, dst, send, recv, device):
        return pltpu.make_async_remote_copy(
            src_ref=src, dst_ref=dst, send_sem=send, recv_sem=recv, device_id=device, device_id_type=MESH
        )

    def peer_x(d):
        to = (along_x + d) % NX
        return to, (4 * to + 2 * along_y + core, gy)

    mine = aligned(core, half)
    my_rows = aligned(core, depth)
    local = [
        pltpu.make_async_copy(tokens.at[:, aligned(gx, depth)], tok.at[aligned(gx, ROWS)], local_sem.at[0]),
        pltpu.make_async_copy(gate.at[:, mine], wg.at[my_rows], local_sem.at[1]),
        pltpu.make_async_copy(up.at[:, mine], wu.at[my_rows], local_sem.at[2]),
        pltpu.make_async_copy(down, wd, local_sem.at[3]),
    ]
    for copy in local:
        copy.start()
    fin[...] = jnp.zeros_like(fin)

    barrier = pltpu.get_barrier_semaphore()

    def greet(d, carry):
        pl.semaphore_signal(barrier, inc=1, device_id=((gx + d) % N, gy), device_id_type=MESH)
        pl.semaphore_signal(barrier, inc=1, device_id=(gx, (gy + d) % N), device_id_type=MESH)
        return carry

    with jax.named_scope("enter"):
        lax.fori_loop(1, N, greet, 0)
        pl.semaphore_wait(barrier, 2 * (N - 1))

    def token_copy(d):
        to = (gx + d) % N
        return remote(
            tokens.at[:, aligned(to, depth)], tok.at[aligned(gx, ROWS)], tok_send.at[d], tok_recv.at[gx], (to, gy)
        )

    def start_tokens(d, carry):
        token_copy(d).start()
        return carry

    lax.fori_loop(1, N, start_tokens, 0)

    theirs = aligned(1 - core, half)
    weights = [
        remote(gate.at[:, theirs], wg.at[my_rows], w_send.at[0], w_recv.at[0], sibling),
        remote(up.at[:, theirs], wu.at[my_rows], w_send.at[1], w_recv.at[1], sibling),
    ]
    for copy in weights:
        copy.start()

    count = [counts[g] for g in range(N)]
    first = [jnp.int32(0)]
    for g in range(N - 1):
        first.append(first[-1] + count[g])

    def wait_tokens(g, carry):
        @pl.when(g != gx)
        def _():
            remote(tok.at[aligned(g, ROWS)], tok.at[aligned(g, ROWS)], tok_send.at[0], tok_recv.at[g], (g, gy)).wait_recv()

        return carry

    def compact(k):
        lane = lax.broadcasted_iota(I32, (1, SPAN * ROWS), 1)
        place = jnp.full((1, SPAN * ROWS), -1, I32)
        for i in range(SPAN):
            g = 2 * k + i
            slot = lane - ROWS * i
            place = jnp.where((slot >= 0) & (slot < count[g]), slot + (first[g] - M * k), place)
        row = lax.broadcasted_iota(I32, (M, SPAN * ROWS), 0)
        pick = jnp.where(row == place, 1.0, 0.0).astype(BF16)
        rows = jnp.dot(pick, tok[pl.ds(2 * k * ROWS, SPAN * ROWS), :], preferred_element_type=F32)
        xs[k, :, my_rows] = rows.astype(BF16)

    def x_copy(k):
        return remote(xs.at[k, :, my_rows], xs.at[k, :, my_rows], x_send.at[k], x_recv.at[k], sibling)

    local[0].wait()
    for k in range(CHUNKS):
        with jax.named_scope(f"tokens{k}"):
            lax.fori_loop(0 if k == 0 else 2 * k + 4, 2 * k + 6, wait_tokens, 0)
        with jax.named_scope(f"compact{k}"):
            compact(k)
            x_copy(k).start()

    for copy in local[1:3]:
        copy.wait()
    for copy in weights:
        copy.wait_recv()

    def encode(ref, parts):
        top = functools.reduce(jnp.maximum, [jnp.max(jnp.abs(v), axis=1, keepdims=True) for v in parts])
        level = jnp.ceil(jnp.log(jnp.maximum(top, 1e-30)) * (64.0 / 0.6931471805599453)) + 1.0
        to_code = FULL * jnp.exp2(level * (-1.0 / 64.0))
        at = 0
        for v in parts:
            ref[:, at : at + v.shape[1]] = jnp.round(v * to_code).astype(I32).astype(I16)
            at += v.shape[1]
        ref[:, at:] = jnp.broadcast_to(level.astype(I32), (top.shape[0], 128)).astype(I16)

    def decode(ref):
        block = ref[...].astype(I32).astype(F32)
        used = block.shape[-1] - 128
        return block[..., :used] * (jnp.exp2(block[..., used : used + 1] * (1.0 / 64.0)) * (1.0 / FULL))

    def to_x(k, size, rows=None):
        copies = []
        for d in range(1, NX):
            to, device = peer_x(d)
            copies.append((aligned(to if rows is None else rows, size), aligned(along_x, size), d, along_x, device))
        return copies

    def from_x(size):
        return [(aligned(peer_x(d)[0], size), peer_x(d)[0]) for d in range(1, NX)]

    def start_all(copies):
        for copy in copies:
            copy.start()

    def wait_from(ref, semaphore, parts):
        for rows, place in parts:
            remote(ref.at[rows], ref.at[rows], semaphore.at[place], semaphore.at[place], sibling).wait_recv()

    def a_copies(k):
        if TYPES[k] == 0:
            plan = [(aligned(1 - along_y, M // 2), pl.ds(0, M // 2), 0, 0, across)]
        else:
            plan = to_x(k, 2 * MC)
        return [remote(qs.at[k, r], q1.at[k, t], a_send.at[k, i], a_recv.at[k, j], v) for r, t, i, j, v in plan]

    def project(k):
        x_copy(k).wait_recv()
        x = xs[k]
        g = jnp.dot(x, wg[...], preferred_element_type=F32)
        u = jnp.dot(x, wu[...], preferred_element_type=F32)
        encode(qs.at[k], [g, u])
        start_all(a_copies(k))

    def b_copies(k):
        if TYPES[k] == 0:
            plan = to_x(k, MC)
        else:
            plan = [(aligned(1 - along_y, MC), pl.ds(0, MC), 0, 0, across)]
        return [remote(qm.at[k, r], q2.at[k, t], b_send.at[k, i], b_recv.at[k, j], v) for r, t, i, j, v in plan]

    def pair(k):
        if TYPES[k] == 0:
            parts, own, size = [(pl.ds(0, M // 2), 0)], along_y, M // 2
        else:
            parts, own, size = from_x(2 * MC), along_x, 2 * MC
        wait_from(q1.at[k], a_recv.at[k], parts)
        total = decode(qs.at[k, aligned(own, size)])
        for rows, _ in parts:
            total = total + decode(q1.at[k, rows])
        encode(qm.at[k, pl.ds(0, size)], [total])
        start_all(b_copies(k))

    def block_of(k):
        return NX * along_y + along_x if TYPES[k] == 0 else 2 * along_x + along_y

    def h_copies(k):
        block = hid.at[k, aligned(block_of(k), MC), mine]
        if TYPES[k] == 0:
            plan = [(d, along_x, peer_x(d)[1]) for d in range(1, NX)]
        else:
            plan = [(0, 0, across)]
        return [remote(block, block, h_send.at[k, i], h_recv.at[k, j], v) for i, j, v in plan]

    def activate(k):
        if TYPES[k] == 0:
            parts, own = from_x(MC), along_x
        else:
            parts, own = [(pl.ds(0, MC), 0)], along_y
        wait_from(q2.at[k], b_recv.at[k], parts)
        total = decode(qm.at[k, aligned(own, MC)])
        for rows, _ in parts:
            total = total + decode(q2.at[k, rows])
        g, u = total[:, :half], total[:, half:]
        hid[k, aligned(block_of(k), MC), mine] = (g / (1.0 + jnp.exp(-g)) * u).astype(BF16)
        start_all(h_copies(k))

    def held(k):
        return aligned(along_y, M // 2) if TYPES[k] == 0 else aligned(along_x, 2 * MC)

    def g_copies(k):
        block = hid.at[k, held(k), mine]
        if TYPES[k] == 0:
            plan = [(0, 0, across)]
        else:
            plan = [(d, along_x, peer_x(d)[1]) for d in range(1, NX)]
        return [remote(block, block, g_send.at[k, i], g_recv.at[k, j], v) for i, j, v in plan]

    def g_parts(k):
        return [(aligned(1 - along_y, M // 2), 0)] if TYPES[k] == 0 else from_x(2 * MC)

    def f_copies(k):
        spots = [held(k)] + [rows for rows, _ in g_parts(k)]
        return [
            remote(hid.at[k, rows, mine], hid.at[k, rows, mine], f_send.at[k, i], f_recv.at[k, i], sibling)
            for i, rows in enumerate(spots)
        ]

    def spread(k):
        if TYPES[k] == 0:
            parts = [(aligned(NX * along_y + peer_x(d)[0], MC), peer_x(d)[0]) for d in range(1, NX)]
        else:
            parts = [(aligned(2 * along_x + 1 - along_y, MC), 0)]
        wait_from(hid.at[k, :, mine], h_recv.at[k], parts)
        start_all(g_copies(k))
        f_copies(k)[0].start()

    def forward(k):
        for part, copy in zip(g_parts(k), f_copies(k)[1:], strict=True):
            wait_from(hid.at[k, :, mine], g_recv.at[k], [part])
            copy.start()

    def owner(k, i):
        return CHIPS * (i % 2) + (i // 2 * 2 + k % 2 + 4 * (k // 2)) % CHIPS

    def owned(k):
        return (gy + 4 * (k // 2)) % CHIPS // 2 * 2 + gy // CHIPS

    def owns(k):
        return gy % 2 == k % 2

    def z_copy(k, i):
        rows = aligned(i, MZ)
        return remote(zs.at[k, rows], zr.at[k // 2, gy], z_send.at[k, i], z_recv.at[k // 2, gy], (gx, owner(k, i)))

    def contract(k):
        for copy in f_copies(k):
            copy.wait_recv()
        o = jnp.dot(hid[k], wd[...], preferred_element_type=F32)
        part[k] = o
        zs[k] = o.astype(BF16)

        def start_out(i, carry):
            @pl.when(owner(k, i) != gy)
            def _():
                z_copy(k, i).start()

            return carry

        lax.fori_loop(0, OWNERS, start_out, 0)

    def e_copy(k, i):
        block = OWNERS * k + owned(k)
        to = block // 4 + i
        place = block - 4 * to + 16
        return to, place, remote(ecode.at[k // 2], fin.at[place], e_send.at[k // 2, i], e_recv.at[place], (gx, to))

    def e_local_copy(k, place):
        return pltpu.make_async_copy(ecode.at[k // 2], fin.at[place], e_local.at[k // 2])

    def collect(k):
        @pl.when(owns(k))
        def _():
            zk = zr.at[k // 2]

            def add(d, total):
                source = (gy + d) % N
                remote(zk.at[source], zk.at[source], z_send.at[k, 0], z_recv.at[k // 2, source], sibling).wait_recv()
                return total + zk[source].astype(F32)

            total = lax.fori_loop(1, N, add, part[k, aligned(owned(k), MZ), :])
            encode(ecode.at[k // 2], [total])
            for i in range(DEST):
                to, place, copy = e_copy(k, i)

                @pl.when(to == gy)
                def _():
                    e_local_copy(k, place).start()

                @pl.when(to != gy)
                def _():
                    copy.start()

    def run(step, k):
        with jax.named_scope(f"{step.__name__}{k}"):
            step(k)

    steps = (project, pair, activate, spread, forward, contract, collect)
    for step, k in ORDER:
        if (step, k) == (5, 0):
            local[3].wait()
        run(steps[step], k)

    def wait_rows(place, carry):
        block = 4 * gy - 16 + place
        source = owner(block // OWNERS, block % OWNERS)

        @pl.when((block >= 0) & (block < LIVE // MZ) & (source != gy))
        def _():
            remote(ecode.at[0], fin.at[place], e_send.at[0, 0], e_recv.at[place], sibling).wait_recv()

        return carry

    with jax.named_scope("rows"):
        lax.fori_loop(0, WINDOW, wait_rows, 0)
    for k in range(CHUNKS):
        for i in range(DEST):
            to, place, copy = e_copy(k, i)

            @pl.when(owns(k) & (to == gy))
            def _():
                e_local_copy(k, place).wait()

    my_count, my_first = jnp.int32(0), jnp.int32(0)
    for g in range(N):
        my_count = my_count + jnp.where(g == gy, count[g], 0)
        my_first = my_first + jnp.where(g < gy, count[g], 0)
    slot = lax.broadcasted_iota(I32, (ROWS, WINDOW * MZ), 0)
    live = lax.broadcasted_iota(I32, (ROWS, WINDOW * MZ), 1) + (ROWS * gy - 256) - my_first
    pick = jnp.where((live == slot) & (slot < my_count), 1.0, 0.0).astype(BF16)
    rest = decode(fin).reshape(WINDOW * MZ, width)
    total = jnp.zeros((ROWS, width), F32)
    for _ in range(3):
        term = rest.astype(BF16)
        total = total + jnp.dot(pick, term, preferred_element_type=F32)
        rest = rest - term.astype(F32)
    out[...] = total

    for copy in weights:
        copy.wait_send()

    def sent_tokens(d, carry):
        token_copy(d).wait_send()
        return carry

    lax.fori_loop(1, N, sent_tokens, 0)
    for k in range(CHUNKS):
        for copy in [x_copy(k)] + a_copies(k) + b_copies(k) + h_copies(k) + g_copies(k) + f_copies(k):
            copy.wait_send()

        def sent_out(i, carry, k=k):
            @pl.when(owner(k, i) != gy)
            def _():
                z_copy(k, i).wait_send()

            return carry

        lax.fori_loop(0, OWNERS, sent_out, 0)
        for i in range(DEST):
            to, place, copy = e_copy(k, i)

            @pl.when(owns(k) & (to != gy))
            def _():
                copy.wait_send()


def body(tokens, gate, up, down, counts):
    depth, hidden = gate.shape
    width = down.shape[1]
    half = hidden // 2
    code = 2 * half + 128
    dma = pltpu.SemaphoreType.DMA
    any_space = pl.BlockSpec(memory_space=pl.ANY)
    return pl.pallas_call(
        kernel,
        out_shape=jax.ShapeDtypeStruct((ROWS, width), F32),
        in_specs=[pl.BlockSpec(memory_space=pltpu.SMEM)] + [any_space] * 4,
        out_specs=pl.BlockSpec(memory_space=pltpu.VMEM),
        scratch_shapes=[
            pltpu.VMEM((N * ROWS, depth), BF16),
            pltpu.VMEM((2 * depth, half), BF16),
            pltpu.VMEM((2 * depth, half), BF16),
            pltpu.VMEM((hidden, width), BF16),
            pltpu.VMEM((CHUNKS, M, 2 * depth), BF16),
            pltpu.VMEM((CHUNKS, M, code), I16),
            pltpu.VMEM((CHUNKS, M, code), I16),
            pltpu.VMEM((CHUNKS, M // 2, code), I16),
            pltpu.VMEM((CHUNKS, M // 2, code), I16),
            pltpu.VMEM((CHUNKS, M, hidden), BF16),
            pltpu.VMEM((CHUNKS, M, width), F32),
            pltpu.VMEM((CHUNKS, M, width), BF16),
            pltpu.VMEM((CHUNKS // 2, N, MZ, width), BF16),
            pltpu.VMEM((CHUNKS // 2, MZ, width + 128), I16),
            pltpu.VMEM((WINDOW, MZ, width + 128), I16),
            dma((4,)),
            dma((N,)), dma((N,)),
            dma((2,)), dma((2,)),
            dma((CHUNKS,)), dma((CHUNKS,)),
            dma((CHUNKS, NX)), dma((CHUNKS, NX)),
            dma((CHUNKS, NX)), dma((CHUNKS, NX)),
            dma((CHUNKS, NX)), dma((CHUNKS, NX)),
            dma((CHUNKS, NX)), dma((CHUNKS, NX)),
            dma((CHUNKS, NX)), dma((CHUNKS, NX)),
            dma((CHUNKS, OWNERS)), dma((CHUNKS // 2, N)),
            dma((CHUNKS // 2, DEST)), dma((WINDOW,)),
            dma((CHUNKS // 2,)),
        ],
        compiler_params=pltpu.CompilerParams(
            collective_id=0, has_side_effects=True, vmem_limit_bytes=56 * 2**20
        ),
        name="swiglu",
    )(counts, tokens, gate, up, down)


def solution(mesh):
    in_specs = (P("gx", None), P("gx", "gy"), P("gx", "gy"), P("gy", "gx"), P())
    out_specs = P("gy", "gx")
    return jax.shard_map(body, mesh=mesh, in_specs=in_specs, out_specs=out_specs, check_vma=False)
```

time: 113 us -> 97.1 us (0.86)
  Pallas kernels: 111 us -> 95 us
    pallas_call x1, Pallas kernels: 111 us -> 95 us  [body(): pl.pallas_call(kernel, out_shape=jax.ShapeDtypeStruct((ROWS, width), F32)...]
where the time goes in v2:
time: 97.1 us; the launch traced here: 96.6 us
  Pallas kernels  95 us (98%)
  local copies, waits for them, and re-layouts  1.57 us (2%)
    pallas_call x1, Pallas kernels, body(): pl.pallas_call(kernel, out_shape=jax.ShapeDtypeStruct((ROWS, width), F32)...  95 us

profile of v2, /device:TPU:80, one launch (start us, length us, event | category | flops | bytes accessed | tf_op | source)
XLA Modules:
  0.0 96.6 jit_solution(7078307943527508041)
XLA Ops:
  0.0 95.0 %swiglu.1 = f32[64,512]{1,0:T(8,128)} custom-call(s32[16]{0:T(128)} %counts.1, bf16[64,8192]{1,0:T(8,128)(2,1)} %tokens.1, bf16[512,1792]{1,0:T(8,128)(2,1)} %gate.1, bf16[512,1792]{1,0:T(8,128)(2,1)} %up.1, bf16[1792,512]{1,0:T(8,128)(2,1)} %down.1), custom_call_target="tpu_custom_call" | custom-call | tf_op jit(solution)/shard_map/swiglu/pallas_call | solution.py:414
  95.0 1.6 %copy.7 = f32[64,512]{1,0:T(8,128)} copy(f32[64,512]{1,0:T(8,128)} %swiglu.1) | data formatting | bytes 262144

commit v3 on v2

--- a/solution.py
+++ b/solution.py
@@ -15,22 +15,30 @@
 NX = 4
 ROWS = 64
 LIVE = 768
-TYPES = (0, 1, 0, 0, 1, 0)
+TYPES = (1, 1, 0, 0, 0, 0)
 CHUNKS = len(TYPES)
 M = LIVE // CHUNKS
 MC = M // CHIPS
 MZ = 16
 OWNERS = M // MZ
 ORDER = (
-    (0, 0), (0, 1), (0, 2), (0, 3), (0, 4), (0, 5), (1, 0), (1, 1), (1, 2), (1, 4), (2, 0), (1, 3),
-    (2, 2), (3, 0), (1, 5), (2, 3), (2, 1), (3, 2), (2, 4), (4, 0), (2, 5), (3, 1), (3, 3), (5, 0),
-    (4, 2), (3, 5), (3, 4), (5, 2), (4, 1), (4, 3), (5, 1), (5, 3), (6, 0), (4, 4), (4, 5), (5, 4),
-    (6, 2), (5, 5), (6, 1), (6, 3), (6, 4), (6, 5),
+    (7, 3), (7, 0), (7, 1), (0, 3), (0, 1), (7, 2), (0, 2), (7, 5), (1, 3), (7, 4), (0, 0), (1, 1),
+    (0, 4), (2, 1), (2, 3), (1, 2), (1, 0), (3, 1), (3, 3), (1, 4), (2, 0), (0, 5), (4, 3), (2, 2),
+    (3, 0), (4, 1), (5, 3), (5, 1), (2, 4), (3, 2), (1, 5), (4, 0), (3, 4), (5, 0), (4, 2), (2, 5),
+    (5, 2), (4, 4), (3, 5), (5, 4), (4, 5), (5, 5), (6, 3), (6, 0), (6, 2), (6, 4), (6, 1), (6, 5),
 )
 SPAN = 6
 WINDOW = 20
 DEST = 5
 FULL = 32000.0
+
+
+def mod(a, b):
+    return a % b if isinstance(a, int) else lax.rem(a, jnp.int32(b))
+
+
+def div(a, b):
+    return a // b if isinstance(a, int) else lax.div(a, jnp.int32(b))
 
 
 def aligned(index, unit):
@@ -45,7 +53,7 @@
     z_send, z_recv, e_send, e_recv, e_local,
 ):
     gx, gy = lax.axis_index("gx"), lax.axis_index("gy")
-    along_x, along_y, core = gx // 4, gx // 2 % 2, gx % 2
+    along_x, along_y, core = div(gx, 4), mod(div(gx, 2), 2), mod(gx, 2)
     depth = gate.shape[0]
     half = gate.shape[1] // 2
     width = down.shape[1]
@@ -58,7 +66,7 @@
         )
 
     def peer_x(d):
-        to = (along_x + d) % NX
+        to = mod(along_x + d, NX)
         return to, (4 * to + 2 * along_y + core, gy)
 
     mine = aligned(core, half)
@@ -76,8 +84,8 @@
     barrier = pltpu.get_barrier_semaphore()
 
     def greet(d, carry):
-        pl.semaphore_signal(barrier, inc=1, device_id=((gx + d) % N, gy), device_id_type=MESH)
-        pl.semaphore_signal(barrier, inc=1, device_id=(gx, (gy + d) % N), device_id_type=MESH)
+        pl.semaphore_signal(barrier, inc=1, device_id=(mod(gx + d, N), gy), device_id_type=MESH)
+        pl.semaphore_signal(barrier, inc=1, device_id=(gx, mod(gy + d, N)), device_id_type=MESH)
         return carry
 
     with jax.named_scope("enter"):
@@ -85,7 +93,7 @@
         pl.semaphore_wait(barrier, 2 * (N - 1))
 
     def token_copy(d):
-        to = (gx + d) % N
+        to = mod(gx + d, N)
         return remote(
             tokens.at[:, aligned(to, depth)], tok.at[aligned(gx, ROWS)], tok_send.at[d], tok_recv.at[gx], (to, gy)
         )
@@ -132,17 +140,15 @@
         return remote(xs.at[k, :, my_rows], xs.at[k, :, my_rows], x_send.at[k], x_recv.at[k], sibling)
 
     local[0].wait()
-    for k in range(CHUNKS):
-        with jax.named_scope(f"tokens{k}"):
-            lax.fori_loop(0 if k == 0 else 2 * k + 4, 2 * k + 6, wait_tokens, 0)
-        with jax.named_scope(f"compact{k}"):
-            compact(k)
-            x_copy(k).start()
-
-    for copy in local[1:3]:
-        copy.wait()
-    for copy in weights:
-        copy.wait_recv()
+    seen = set()
+
+    def arrange(k):
+        for g in range(2 * k, 2 * k + SPAN):
+            if g not in seen:
+                seen.add(g)
+                wait_tokens(g, 0)
+        compact(k)
+        x_copy(k).start()
 
     def encode(ref, parts):
         top = functools.reduce(jnp.maximum, [jnp.max(jnp.abs(v), axis=1, keepdims=True) for v in parts])
@@ -271,13 +277,13 @@
             copy.start()
 
     def owner(k, i):
-        return CHIPS * (i % 2) + (i // 2 * 2 + k % 2 + 4 * (k // 2)) % CHIPS
+        return CHIPS * mod(i, 2) + mod(div(i, 2) * 2 + mod(k, 2) + 4 * div(k, 2), CHIPS)
 
     def owned(k):
-        return (gy + 4 * (k // 2)) % CHIPS // 2 * 2 + gy // CHIPS
+        return div(mod(gy + 4 * (k // 2), CHIPS), 2) * 2 + div(gy, CHIPS)
 
     def owns(k):
-        return gy % 2 == k % 2
+        return mod(gy, 2) == k % 2
 
     def z_copy(k, i):
         rows = aligned(i, MZ)
@@ -290,18 +296,15 @@
         part[k] = o
         zs[k] = o.astype(BF16)
 
-        def start_out(i, carry):
-            @pl.when(owner(k, i) != gy)
-            def _():
-                z_copy(k, i).start()
-
+        def start_out(j, carry):
+            z_copy(k, mod(owned(k) + j, OWNERS)).start()
             return carry
 
-        lax.fori_loop(0, OWNERS, start_out, 0)
+        lax.fori_loop(jnp.where(owns(k), 1, 0), OWNERS, start_out, 0)
 
     def e_copy(k, i):
         block = OWNERS * k + owned(k)
-        to = block // 4 + i
+        to = div(block, 4) + i
         place = block - 4 * to + 16
         return to, place, remote(ecode.at[k // 2], fin.at[place], e_send.at[k // 2, i], e_recv.at[place], (gx, to))
 
@@ -314,7 +317,7 @@
             zk = zr.at[k // 2]
 
             def add(d, total):
-                source = (gy + d) % N
+                source = mod(gy + d, N)
                 remote(zk.at[source], zk.at[source], z_send.at[k, 0], z_recv.at[k // 2, source], sibling).wait_recv()
                 return total + zk[source].astype(F32)
 
@@ -331,19 +334,21 @@
                 def _():
                     copy.start()
 
-    def run(step, k):
-        with jax.named_scope(f"{step.__name__}{k}"):
-            step(k)
-
-    steps = (project, pair, activate, spread, forward, contract, collect)
+    steps = (project, pair, activate, spread, forward, contract, collect, arrange)
     for step, k in ORDER:
-        if (step, k) == (5, 0):
+        if (step, k) == (0, 3):
+            for copy in local[1:3]:
+                copy.wait()
+            for copy in weights:
+                copy.wait_recv()
+        if (step, k) == (5, 3):
             local[3].wait()
-        run(steps[step], k)
+        steps[step](k)
 
     def wait_rows(place, carry):
         block = 4 * gy - 16 + place
-        source = owner(block // OWNERS, block % OWNERS)
+        at = jnp.maximum(block, 0)
+        source = owner(div(at, OWNERS), mod(at, OWNERS))
 
         @pl.when((block >= 0) & (block < LIVE // MZ) & (source != gy))
         def _():
@@ -388,14 +393,11 @@
         for copy in [x_copy(k)] + a_copies(k) + b_copies(k) + h_copies(k) + g_copies(k) + f_copies(k):
             copy.wait_send()
 
-        def sent_out(i, carry, k=k):
-            @pl.when(owner(k, i) != gy)
-            def _():
-                z_copy(k, i).wait_send()
-
+        def sent_out(j, carry, k=k):
+            z_copy(k, mod(owned(k) + j, OWNERS)).wait_send()
             return carry
 
-        lax.fori_loop(0, OWNERS, sent_out, 0)
+        lax.fori_loop(jnp.where(owns(k), 1, 0), OWNERS, sent_out, 0)
         for i in range(DEST):
             to, place, copy = e_copy(k, i)
 

time: 97.1 us -> 94.9 us (0.977)
  the two profiles are of different devices: /device:TPU:80 before, /device:TPU:25 now
where the time goes in v3:
time: 94.9 us; the launch traced here: 94.8 us
  Pallas kernels  93.2 us (98%)
  local copies, waits for them, and re-layouts  1.57 us (2%)
    pallas_call x1, Pallas kernels, body(): pl.pallas_call(kernel, out_shape=jax.ShapeDtypeStruct((ROWS, width), F32)...  93.2 us

profile of v3, /device:TPU:25, one launch (start us, length us, event | category | flops | bytes accessed | tf_op | source)
XLA Modules:
  0.0 94.8 jit_solution(14350929432064370145)
XLA Ops:
  0.0 93.2 %swiglu.1 = f32[64,512]{1,0:T(8,128)} custom-call(s32[16]{0:T(128)} %counts.1, bf16[64,8192]{1,0:T(8,128)(2,1)} %tokens.1, bf16[512,1792]{1,0:T(8,128)(2,1)} %gate.1, bf16[512,1792]{1,0:T(8,128)(2,1)} %up.1, bf16[1792,512]{1,0:T(8,128)(2,1)} %down.1), custom_call_target="tpu_custom_call" | custom-call | tf_op jit(solution)/shard_map/swiglu/pallas_call | solution.py:416
  93.2 1.6 %copy.7 = f32[64,512]{1,0:T(8,128)} copy(f32[64,512]{1,0:T(8,128)} %swiglu.1) | data formatting | bytes 262144

commit v4 on v3

--- a/solution.py
+++ b/solution.py
@@ -15,17 +15,17 @@
 NX = 4
 ROWS = 64
 LIVE = 768
-TYPES = (1, 1, 0, 0, 0, 0)
+TYPES = (1, 0, 1, 0, 0, 0)
 CHUNKS = len(TYPES)
 M = LIVE // CHUNKS
 MC = M // CHIPS
 MZ = 16
 OWNERS = M // MZ
 ORDER = (
-    (7, 3), (7, 0), (7, 1), (0, 3), (0, 1), (7, 2), (0, 2), (7, 5), (1, 3), (7, 4), (0, 0), (1, 1),
-    (0, 4), (2, 1), (2, 3), (1, 2), (1, 0), (3, 1), (3, 3), (1, 4), (2, 0), (0, 5), (4, 3), (2, 2),
-    (3, 0), (4, 1), (5, 3), (5, 1), (2, 4), (3, 2), (1, 5), (4, 0), (3, 4), (5, 0), (4, 2), (2, 5),
-    (5, 2), (4, 4), (3, 5), (5, 4), (4, 5), (5, 5), (6, 3), (6, 0), (6, 2), (6, 4), (6, 1), (6, 5),
+    (7, 1), (7, 3), (7, 4), (7, 2), (0, 1), (0, 3), (0, 2), (7, 0), (1, 1), (7, 5), (0, 0), (1, 2),
+    (0, 5), (2, 1), (1, 3), (2, 2), (1, 0), (1, 5), (3, 1), (3, 2), (2, 0), (0, 4), (4, 1), (2, 5),
+    (3, 0), (5, 1), (2, 3), (4, 2), (3, 5), (5, 2), (1, 4), (4, 0), (5, 0), (3, 3), (4, 5), (2, 4),
+    (5, 5), (4, 3), (3, 4), (5, 3), (4, 4), (6, 2), (6, 1), (5, 4), (6, 5), (6, 3), (6, 0), (6, 4),
 )
 SPAN = 6
 WINDOW = 20
@@ -336,12 +336,12 @@
 
     steps = (project, pair, activate, spread, forward, contract, collect, arrange)
     for step, k in ORDER:
-        if (step, k) == (0, 3):
+        if (step, k) == (0, 1):
             for copy in local[1:3]:
                 copy.wait()
             for copy in weights:
                 copy.wait_recv()
-        if (step, k) == (5, 3):
+        if (step, k) == (5, 1):
             local[3].wait()
         steps[step](k)
 

time: 94.9 us -> 97.5 us (1.027)
  the two profiles are of different devices: /device:TPU:25 before, /device:TPU:80 now
where the time goes in v4:
time: 97.5 us; the launch traced here: 96.9 us
  Pallas kernels  95.4 us (98%)
  local copies, waits for them, and re-layouts  1.57 us (2%)
    pallas_call x1, Pallas kernels, body(): pl.pallas_call(kernel, out_shape=jax.ShapeDtypeStruct((ROWS, width), F32)...  95.4 us

profile of v4, /device:TPU:80, one launch (start us, length us, event | category | flops | bytes accessed | tf_op | source)
XLA Modules:
  0.0 96.9 jit_solution(3223920425549875263)
XLA Ops:
  0.0 95.4 %swiglu.1 = f32[64,512]{1,0:T(8,128)} custom-call(s32[16]{0:T(128)} %counts.1, bf16[64,8192]{1,0:T(8,128)(2,1)} %tokens.1, bf16[512,1792]{1,0:T(8,128)(2,1)} %gate.1, bf16[512,1792]{1,0:T(8,128)(2,1)} %up.1, bf16[1792,512]{1,0:T(8,128)(2,1)} %down.1), custom_call_target="tpu_custom_call" | custom-call | tf_op jit(solution)/shard_map/swiglu/pallas_call | solution.py:416
  95.4 1.6 %copy.7 = f32[64,512]{1,0:T(8,128)} copy(f32[64,512]{1,0:T(8,128)} %swiglu.1) | data formatting | bytes 262144
